TPU v7x, 32 devices: a whole 2x2x4 slice. The times are simulated.
32 devices in a mesh: row: 4 (over y, x), col: 8 (over z, core).
Axes of the slice: x: 2, y: 2, z: 4, core: 2. Of those that a mesh axis runs over, the one named last changes fastest.
Arguments:
- adj_tiles: bfloat16 [4, 8, 20, 256, 256], P('row', 'col'), may hold values from -0.125 to 0.125
- tile_rows: int32 [4, 8, 20], P('row', 'col'), may hold values from 0 to 7, as said below
- tile_cols: int32 [4, 8, 20], P('row', 'col'), may hold values from 0 to 3
- tile_counts: int32 [4, 8], P('row', 'col'), may hold values from 5 to 20, as said below
- features: bfloat16 [8192, 512], P(('col', 'row')), may hold values from -6 to 6
- weight: bfloat16 [512, 512], replicated, may hold values from -0.25 to 0.25
- node_grad: bfloat16 [8192, 512], P(('row', 'col')), may hold values from -6 to 6
Outputs:
- node_out: bfloat16 [8192, 512], P(('row', 'col'))
- weight_grad: float32 [512, 512], replicated
- feature_grad: bfloat16 [8192, 512], P(('col', 'row'))
Inputs may be any that keep to these rules, and one draw needn't show every extreme that they name: Within one cell the first 20 slots name distinct tiles (pairs of tile_rows and tile_cols). `tile_counts`: slots from this number on hold no tile; some cell fills all its slots.
All inputs are finite; a program needn't handle non-finite values.
Results may differ from a plain program's by a relative error of at most 0.027.
Values may be sent and summed in bfloat16 or wider, within the bound.
A program may use at most 128 MiB of HBM per device.

v0:
```python
import jax
import jax.numpy as jnp
from jax import lax
from jax.sharding import PartitionSpec as P


def spread_tiles(
    cell_tiles,
    order,
    dest_ids,
    source_ids,
    first_live,
    end_live,
    source,
    dest_first,
    dest_tiles,
    transposed,
):
    slot_total = cell_tiles.shape[0]
    slot_block = min(16, slot_total)
    tile_size = cell_tiles.shape[1]
    feat_width = source.shape[2]
    block_total = (end_live - first_live + slot_block - 1) // slot_block
    slot_range = jnp.arange(slot_block, dtype=jnp.int32)
    dest_range = jnp.arange(dest_tiles, dtype=jnp.int32)

    def add_block(block_index, running):
        positions = first_live + block_index * slot_block + slot_range
        live_slots = positions < end_live
        clamped = jnp.minimum(positions, slot_total - 1)
        slot_ids = jnp.take(order, clamped, axis=0)
        tile_block = jnp.take(cell_tiles, slot_ids, axis=0)
        dest_block = jnp.take(dest_ids, slot_ids, axis=0)
        source_block = jnp.take(source_ids, slot_ids, axis=0)
        source_pieces = jnp.take(source, source_block, axis=0)
        if transposed:
            products = jnp.einsum(
                "sba,sbf->saf", tile_block, source_pieces, preferred_element_type=jnp.float32
            )
        else:
            products = jnp.einsum(
                "sab,sbf->saf", tile_block, source_pieces, preferred_element_type=jnp.float32
            )
        placing = (dest_range[:, None] == (dest_block - dest_first)[None, :]) & live_slots[None, :]
        placing = placing.astype(jnp.float32)
        added = jnp.einsum(
            "ds,saf->daf",
            placing,
            products,
            precision=lax.Precision.HIGHEST,
            preferred_element_type=jnp.float32,
        )
        return running + added

    start_value = jnp.zeros((dest_tiles, tile_size, feat_width), jnp.float32)
    return lax.fori_loop(0, block_total, add_block, start_value)


def local(adj_tiles, tile_rows, tile_cols, tile_counts, features, weight, node_grad):
    cell_tiles = adj_tiles[0, 0]
    cell_rows = tile_rows[0, 0]
    cell_cols = tile_cols[0, 0]
    slot_count = tile_counts[0, 0]
    slot_total = cell_tiles.shape[0]
    tile_size = cell_tiles.shape[1]
    feat_width = features.shape[1]
    node_count = features.shape[0]
    row_devices = lax.axis_size("row")
    col_devices = lax.axis_size("col")
    row_tiles = node_count * col_devices // tile_size
    col_tiles = node_count * row_devices // tile_size
    plain_order = jnp.arange(slot_total, dtype=jnp.int32)
    column_feats = lax.all_gather(features, "row", axis=0, tiled=True)
    source = column_feats.reshape(col_tiles, tile_size, feat_width)
    partial_value = spread_tiles(
        cell_tiles, plain_order, cell_rows, cell_cols, 0, slot_count, source, 0, row_tiles, False
    )
    agg = lax.psum_scatter(
        partial_value.reshape(row_tiles * tile_size, feat_width).astype(jnp.bfloat16),
        "col",
        scatter_dimension=0,
        tiled=True,
    )
    pre = jnp.dot(agg, weight, preferred_element_type=jnp.float32)
    node_out = jax.nn.silu(pre).astype(jnp.bfloat16)
    sigma = jax.nn.sigmoid(pre)
    dpre = (node_grad.astype(jnp.float32) * sigma * (1.0 + pre * (1.0 - sigma))).astype(
        jnp.bfloat16
    )
    scale_factor = 1.0 / jnp.sqrt(jnp.float32(node_count * row_devices * col_devices))
    weight_term = jnp.dot(agg.T, dpre, preferred_element_type=jnp.float32) * scale_factor
    dagg = jnp.dot(dpre, weight.T, preferred_element_type=jnp.float32).astype(jnp.bfloat16)
    grad_block = lax.all_gather(dagg, "col", axis=0, tiled=True)
    grad_source = grad_block.reshape(row_tiles, tile_size, feat_width)
    partial_back = spread_tiles(
        cell_tiles,
        plain_order,
        cell_cols,
        cell_rows,
        0,
        slot_count,
        grad_source,
        0,
        col_tiles,
        True,
    )
    summed = lax.psum_scatter(
        partial_back.reshape(col_tiles * tile_size, feat_width).astype(jnp.bfloat16),
        "row",
        scatter_dimension=0,
        tiled=True,
    )
    weight_grad = lax.psum(weight_term, ("row", "col"))
    return (node_out, weight_grad, summed)


def solution(mesh):
    in_specs = (
        P("row", "col", None, None, None),
        P("row", "col", None),
        P("row", "col", None),
        P("row", "col"),
        P(("col", "row"), None),
        P(),
        P(("row", "col"), None),
    )
    out_specs = (P(("row", "col"), None), P(), P(("col", "row"), None))
    return jax.shard_map(local, mesh=mesh, in_specs=in_specs, out_specs=out_specs, check_vma=False)
```

profile of v0, /device:TPU:0, one launch (start us, length us, event | category | flops | bytes accessed | tf_op | source)
XLA Modules:
  0.0 349.4 jit_solution(2514869074892325906)
XLA Ops:
  7.2 0.7 all-gather.3.cloned.1.call-update
  8.6 30.6 %all-gather.3.cloned.1.call-done = bf16[1024,512]{1,0:T(8,128)(2,1)} async-done(((bf16[256,512]{1,0:T(8,128)(2,1)}), bf16[1024,512]{1,0:T(8,128)(2,1)}) %all-gather.3.cloned.1.call-update) | async-done | bytes 1048592 | tf_op jit(solution)/shard_map/all_gather | solution.py:73
  39.2 2.5 broadcast_in_dim.48
  41.7 30.9 %while.22 = (s32[]{:T(128)}, f32[8,256,512]{2,0,1:T(8,128)}, s32[]{:T(128)}, s32[20]{0:T(128)S(1)}, s32[]{:T(128)}, /*index=5*/bf16[20,256,256]{2,1,0:T(8,128)(2...) while((s32[]{:T(128)}, f32[8,256,512]{2,0,1:T(8,128)}, s32[]{:T(128)}, ...), condition=%wide.region_1.0_spmd.clone, body=%wide.region_0.3_spmd.clone.sunk | while | flops 1279266560 | bytes 44054316 | solution.py:56
  41.8 0.7 gather_fusion
  42.4 0.7 compare_and_fusion.8
  43.1 0.7 gather_fusion.1
  43.8 2.8 gather_fusion.2
  46.6 3.8 %gather_fusion.3 = bf16[16,256,256]{2,1,0:T(8,128)(2,1)} fusion(bf16[20,256,256]{2,1,0:T(8,128)(2,1)} %get-tuple-element.354, s32[1024]{0:T(1024)S(1)} %pad_clamp_fusion.13), kind=kCustom, calls=%fused_computation.1.clone.clone.1 | custom fusion | bytes 4194368 | tf_op jit(solution)/shard_map/while/body/jit(_take)/gather | solution.py:32
  50.3 7.4 %fusion.72 = f32[16,256,512]{2,1,0:T(8,128)} fusion(bf16[16,256,512]{2,1,0:T(8,128)(2,1)} %gather_fusion.2, pred[16]{0:T(512)(128)(4,1)S(1)} %get-tuple-element.313, bf16[16,256,256]{2,1,0:T(8,128)(2,1)} %gather_fusion.3, pred[16]{0:T(512)(128)(4,1)S(1)} %get-tuple-element.314), kind=kOutput, calls=%fused_computation.18.clone.1 | convolution fusion | flops 1076887552 | bytes 14680096 | tf_op jit(solution)/shard_map/while/body/sab,sbf->saf/dot_general | solution.py:41
  57.7 0.7 gather_fusion.4
  58.4 14.1 %fusion.73 = f32[8,256,512]{2,0,1:T(8,128)} fusion(f32[8,256,512]{2,0,1:T(8,128)} %get-tuple-element.340, f32[16,256,512]{2,1,0:T(8,128)} %fusion.72, s32[16]{0:T(128)S(1)} %broadcast_select_fusion.4, pred[16]{0:T(512)(128)(4,1)S(1)} %get-tuple-element.315), kind=kOutput, calls=%fused_computation.21.clone.1 | convolution fusion | flops 202375424 | bytes 16777296 | tf_op jit(solution)/shard_map/while/body/ds,saf->daf/dot_general | solution.py:46
  72.6 5.8 %copy.24 = bf16[8,256,512]{2,1,0:T(8,128)(2,1)} copy(f32[8,256,512]{2,0,1:T(8,128)} %get-tuple-element.121) | data formatting | bytes 6291456 | tf_op jit(solution)/shard_map/while | solution.py:56
  78.4 65.8 %reduce-scatter.3.cloned.1.call-done = bf16[256,512]{1,0:T(8,128)(2,1)} async-done(((bf16[2048,512]{1,0:T(8,128)(2,1)}), bf16[256,512]{1,0:T(8,128)(2,1)}) %reduce-scatter.3.cloned.1.call-update) | async-done | bytes 262160 | tf_op jit(solution)/shard_map/reduce_scatter | solution.py:78
  144.3 2.1 multiply_convert_fusion.1
  146.4 1.1 convolution_convert_fusion
  147.5 1.5 convolution_multiply_fusion
  149.1 26.3 %all-gather.5.cloned.1.call-done = bf16[2048,512]{1,0:T(8,128)(2,1)} async-done(((bf16[256,512]{1,0:T(8,128)(2,1)}), bf16[2048,512]{1,0:T(8,128)(2,1)}) %all-gather.5.cloned.1.call-update) | async-done | bytes 2097168 | tf_op jit(solution)/shard_map/all_gather | solution.py:93
  175.3 1.6 broadcast_in_dim.49
  176.9 29.5 %while.23 = (s32[]{:T(128)}, f32[4,256,512]{2,0,1:T(4,128)}, s32[]{:T(128)}, s32[20]{0:T(128)S(1)}, s32[]{:T(128)}, /*index=5*/bf16[20,256,256]{2,1,0:T(8,128)(2...) while((s32[]{:T(128)}, f32[4,256,512]{2,0,1:T(4,128)}, s32[]{:T(128)}, ...), condition=%wide.region_5.8_spmd.clone, body=%wide.region_4.7_spmd.clone.sunk | while | flops 1178078848 | bytes 39860012 | solution.py:56
  176.9 0.7 gather_fusion.5
  177.6 0.7 compare_and_fusion.10
  178.3 0.7 gather_fusion.6
  179.0 4.4 %gather_fusion.7 = bf16[16,256,512]{2,1,0:T(8,128)(2,1)} fusion(bf16[8,256,512]{2,1,0:T(8,128)(2,1)} %get-tuple-element.386, s32[1024]{0:T(1024)S(1)} %pad_clamp_fusion.17), kind=kCustom, calls=%fused_computation.9.clone.clone.1 | custom fusion | bytes 8388672 | tf_op jit(solution)/shard_map/while/body/jit(_take)/gather | solution.py:35
  183.3 2.4 gather_fusion.8
  185.8 6.9 %fusion.78 = f32[16,256,512]{2,1,0:T(8,128)} fusion(bf16[16,256,512]{2,1,0:T(8,128)(2,1)} %gather_fusion.7, pred[16]{0:T(512)(128)(4,1)S(1)} %get-tuple-element.326, bf16[16,256,256]{2,1,0:T(8,128)(2,1)S(1)} %gather_fusion.8, pred[16]{0:T(512)(128)(4,1)S(1)} %get-tuple-element.327), kind=kOutput, calls=%fused_computation.47.clone.1 | convolution fusion | flops 1076887552 | bytes 14680096 | tf_op jit(solution)/shard_map/while/body/sba,sbf->saf/dot_general | solution.py:37
  193.3 13.1 %fusion.79 = f32[4,256,512]{2,0,1:T(4,128)} fusion(f32[4,256,512]{2,0,1:T(4,128)} %get-tuple-element.370, f32[16,256,512]{2,1,0:T(8,128)} %fusion.78, s32[16]{0:T(128)S(1)} %broadcast_select_fusion.5, pred[16]{0:T(512)(128)(4,1)S(1)} %get-tuple-element.328), kind=kOutput, calls=%fused_computation.53.clone.1 | convolution fusion | flops 101187712 | bytes 12582992 | tf_op jit(solution)/shard_map/while/body/ds,saf->daf/dot_general | solution.py:46
  206.4 2.0 convert_element_type.32
  208.4 1.2 copy.12
  209.6 100.7 %all-reduce.2.cloned.1.call-done = f32[512,512]{1,0:T(8,128)} async-done(((f32[512,512]{1,0:T(8,128)}), f32[512,512]{1,0:T(8,128)}) %all-reduce.2.cloned.1.call-update) | async-done | bytes 1048592 | tf_op jit(solution)/shard_map/psum | solution.py:113
  310.3 30.3 %reduce-scatter.5.cloned.1.call-done = bf16[256,512]{1,0:T(8,128)(2,1)} async-done(((bf16[1024,512]{1,0:T(8,128)(2,1)}), bf16[256,512]{1,0:T(8,128)(2,1)}) %reduce-scatter.5.cloned.1.call-update) | async-done | bytes 262160 | tf_op jit(solution)/shard_map/reduce_scatter | solution.py:107
  340.6 2.3 copy.45
  (36 shorter events, 1.0 us)
Async XLA Ops:
  7.2 137.1 %copy-start = (bf16[512,512]{1,0:T(8,128)(2,1)S(1)}, bf16[512,512]{1,0:T(8,128)(2,1)}, u32[]{:S(2)}) copy-start(bf16[512,512]{1,0:T(8,128)(2,1)} %param.20) | copy-start | bytes 1572868
  7.2 34.5 %copy-start.1 = (s32[1,1,20]{2,1,0:T(1,128)S(1)}, s32[1,1,20]{2,1,0:T(1,128)}, u32[]{:S(2)}) copy-start(s32[1,1,20]{2,1,0:T(1,128)} %param.16) | copy-start | bytes 244
  7.2 34.5 %copy-start.2 = (s32[1,1,20]{2,1,0:T(1,128)S(1)}, s32[1,1,20]{2,1,0:T(1,128)}, u32[]{:S(2)}) copy-start(s32[1,1,20]{2,1,0:T(1,128)} %param.17) | copy-start | bytes 244
  7.2 32.0 %all-gather.3.cloned.1.call-start = ((), (), s32[]{:S(2)}) async-start(), calls=%async_computation.2 | async-start | bytes 1310720 | tf_op jit(solution)/shard_map/all_gather | solution.py:73
  7.9 136.3 %reduce-scatter.3.cloned.1.call-start = ((), (), s32[]{:S(2)}) async-start(), calls=%async_computation.3 | async-start | bytes 2359296 | tf_op jit(solution)/shard_map/reduce_scatter | solution.py:78
  39.2 2.5 copy-start.3
  72.6 73.8 %copy-start.4 = (bf16[256,512]{1,0:T(8,128)(2,1)S(1)}, bf16[256,512]{1,0:T(8,128)(2,1)}, u32[]{:S(2)}) copy-start(bf16[256,512]{1,0:T(8,128)(2,1)} %param.21) | copy-start | bytes 786436
  78.4 96.9 %all-gather.5.cloned.1.call-start = ((), (), s32[]{:S(2)}) async-start(), calls=%async_computation.5 | async-start | bytes 2359296 | tf_op jit(solution)/shard_map/all_gather | solution.py:93
  144.2 3.3 copy-start.5
  147.5 162.8 %all-reduce.2.cloned.1.call-start = ((), (), s32[]{:S(2)}) async-start(), calls=%async_computation.4 | async-start | bytes 2097152 | tf_op jit(solution)/shard_map/psum | solution.py:113
  149.0 191.6 %reduce-scatter.5.cloned.1.call-start = ((), (), s32[]{:S(2)}) async-start(), calls=%async_computation.6 | async-start | bytes 1310720 | tf_op jit(solution)/shard_map/reduce_scatter | solution.py:107
Sparse Core Ops, SparseCore 0:
  9.9 29.3 all-gather.2
  78.5 65.6 reduce-scatter.2
  147.6 27.7 all-gather.4
  180.9 129.3 all-reduce.1
  313.9 26.6 reduce-scatter.4
where the time goes:
time: 350 us; the launch traced here: 349 us
  waiting for transfers between devices  254 us (73%)
  matrix products  46.2 us (13%)
  local copies, waits for them, and re-layouts  30.6 us (9%)
  between operations  14.5 us (4%)
    psum x1, waiting for transfers between devices, local(): weight_grad = lax.psum(weight_term, ('row', 'col'))  101 us
    reduce_scatter x1, waiting for transfers between devices, local(): lax.psum_scatter(partial_value.reshape(row_tiles * tile_size, feat_width)...  65.8 us
    all_gather x1, waiting for transfers between devices, local(): column_feats = lax.all_gather(features, 'row', axis=0, tiled=True)  30.6 us
    reduce_scatter x1, waiting for transfers between devices, local(): lax.psum_scatter(partial_back.reshape(col_tiles * tile_size, feat_width)....  30.3 us
    dot_general x2, matrix products, add_block(): jnp.einsum('ds,saf->daf', placing, products, precision=lax.Precision.HIGH...  27.3 us
    all_gather x1, waiting for transfers between devices, local(): grad_block = lax.all_gather(dagg, 'col', axis=0, tiled=True)  26.3 us
    dot_general x1, matrix products, add_block(): jnp.einsum('sab,sbf->saf', tile_block, source_pieces, preferred_element_t...  7.4 us
    gather x2, local copies, waits for them, and re-layouts, add_block(): source_pieces = jnp.take(source, source_block, axis=0)  7.18 us
  transfers between devices with their start and end apart: 5, of which 5 were waited for; matrix products, arithmetic and copies ran while one was open for 10% of the time, Pallas kernels for 0%

commit v1 on v0

v1 whole, which is shorter than its diff:
```python
import functools

import jax
import jax.numpy as jnp
from jax import lax
from jax.experimental import pallas as pl
from jax.experimental.pallas import tpu as pltpu
from jax.sharding import PartitionSpec as P

BF = jnp.bfloat16
F32 = jnp.float32
HALVES = 2


def dot(a, b):
    return jnp.dot(a, b, preferred_element_type=F32)


def kernel(
    R,
    C,
    scale,
    rows_s,
    cols_s,
    count_s,
    adj_hbm,
    feat,
    weight,
    ngrad,
    out,
    wout,
    fgrad,
    adj,
    place,
    denseT,
    feats,
    chip,
    sib_send,
    sib_recv,
    up_recv,
    dn_recv,
    agg,
    dpre_v,
    grads,
    b_send,
    b_recv,
    wterm,
    w1_send,
    w1_recv,
    w1_sum,
    w2_send,
    w2_recv,
    wslab,
    wfull,
    adj_sem,
    f_s,
    f_r,
    sib_s,
    sib_r,
    up_s,
    up_r,
    dn_s,
    dn_r,
    gsib_s,
    gsib_r,
    gup_s,
    gup_r,
    gdn_s,
    gdn_r,
    b_s,
    b_r,
    w1_s,
    w1_r,
    w2_s,
    w2_r,
    w3_s,
    w3_r,
    w4_s,
    w4_r,
):
    H = HALVES
    Z = C // 2
    T, F = feat.shape
    W = F // H
    slots = adj.shape[0] - 1
    i = lax.axis_index("row")
    j = lax.axis_index("col")
    z = j // 2
    c = lax.rem(j, 2)
    sibling = 2 * z + 1 - c
    pending = []

    def remote(src, dst, ssem, rsem, row, col):
        return pltpu.make_async_remote_copy(
            src_ref=src,
            dst_ref=dst,
            send_sem=ssem,
            recv_sem=rsem,
            device_id=(row, col),
            device_id_type=pl.DeviceIdType.MESH,
        )

    def send(copy, cond=None):
        if cond is None:
            copy.start()
        else:
            pl.when(cond)(copy.start)
        pending.append((copy, cond))

    adj_copy = pltpu.make_async_copy(adj_hbm.at[0, 0], adj.at[pl.ds(0, slots)], adj_sem)
    adj_copy.start()

    barrier = pltpu.get_barrier_semaphore()
    for q in range(1, R):
        pl.semaphore_signal(
            barrier, inc=1, device_id=(lax.rem(i + q, R), j), device_id_type=pl.DeviceIdType.MESH
        )
    for q in range(1, C):
        pl.semaphore_signal(
            barrier, inc=1, device_id=(i, lax.rem(j + q, C)), device_id_type=pl.DeviceIdType.MESH
        )
    pl.semaphore_wait(barrier, R + C - 2)

    def tile_at(index):
        return pl.ds(pl.multiple_of(index * T, T), T)

    def feat_copy(h, q):
        return remote(
            feat.at[:, pl.ds(h * W, W)],
            feats.at[h, tile_at(i), :],
            f_s.at[h, q - 1],
            f_r.at[h, q - 1],
            lax.rem(i + q, R),
            j,
        )

    for h in range(H):
        for q in range(1, R):
            send(feat_copy(h, q))
    for h in range(H):
        feats[h, tile_at(i), :] = feat[:, pl.ds(h * W, W)]

    adj[slots] = jnp.zeros((T, T), BF)
    adj_copy.wait()
    count = count_s[0, 0]

    def fill(r, carry):
        for k in range(R):
            found = jnp.int32(slots)
            for t in range(slots):
                hit = (rows_s[0, 0, t] == r) & (cols_s[0, 0, t] == k) & (t < count)
                found = jnp.where(hit, jnp.int32(t), found)
            place[r * R + k] = found
            denseT[k, :, tile_at(r)] = adj[found].T
        return carry

    lax.fori_loop(0, C, fill, 0)

    order = []
    for s in range((Z + 1) // 2):
        order.append(Z - 1 - s)
        if s != Z - 1 - s:
            order.append(s)

    def sib_copy(h, d):
        return remote(
            sib_send.at[h, d], sib_recv.at[h, d], sib_s.at[h, d], sib_r.at[h, d], i, sibling
        )

    def cell_rows(h, r):
        acc = dot(adj[place[r * R]], feats[h, :T, :])
        for k in range(1, R):
            acc = acc + dot(adj[place[r * R + k]], feats[h, k * T : (k + 1) * T, :])
        return acc

    def forward(h):
        for q in range(1, R):
            feat_copy(h, q).wait_recv()
        for d in order:
            sib_send[h, d] = cell_rows(h, 2 * d + 1 - c).astype(BF)
            send(sib_copy(h, d))
        for d in order:
            part = cell_rows(h, 2 * d + c)
            sib_copy(h, d).wait_recv()
            chip[h, d] = (part + sib_recv[h, d].astype(F32)).astype(BF)

    above = jnp.minimum(z + 1, Z - 1)
    below = jnp.maximum(z - 1, 0)

    def up_copy(h, s):
        return remote(
            chip.at[h, Z - 1 - s], up_recv.at[h, s], up_s.at[h, s], up_r.at[h, s], i, 2 * above + c
        )

    def dn_copy(h, s):
        return remote(
            chip.at[h, s], dn_recv.at[h, s], dn_s.at[h, s], dn_r.at[h, s], i, 2 * below + c
        )

    def chain(h, s):
        d = Z - 1 - s

        @pl.when((z > 0) & (z < d))
        def _():
            up_copy(h, s).wait_recv()
            chip[h, d] = (chip[h, d].astype(F32) + up_recv[h, s].astype(F32)).astype(BF)

        send(up_copy(h, s), z < d)

        @pl.when((z < Z - 1) & (z > s))
        def _():
            dn_copy(h, s).wait_recv()
            chip[h, s] = (chip[h, s].astype(F32) + dn_recv[h, s].astype(F32)).astype(BF)

        send(dn_copy(h, s), z > s)

    def finish(h):
        cols = pl.ds(h * W, W)

        @pl.when(z == 0)
        def _():
            dn_copy(h, z).wait_recv()
            agg[:, cols] = (chip[h, z].astype(F32) + dn_recv[h, z].astype(F32)).astype(BF)

        @pl.when(z == Z - 1)
        def _():
            up_copy(h, Z - 1 - z).wait_recv()
            agg[:, cols] = (chip[h, z].astype(F32) + up_recv[h, Z - 1 - z].astype(F32)).astype(BF)

        @pl.when((z > 0) & (z < Z - 1))
        def _():
            up_copy(h, Z - 1 - z).wait_recv()
            dn_copy(h, z).wait_recv()
            both = up_recv[h, Z - 1 - z].astype(F32) + dn_recv[h, z].astype(F32)
            agg[:, cols] = (chip[h, z].astype(F32) + both).astype(BF)

    forward(0)
    for s in range(Z - 2):
        chain(0, s)
    forward(1)
    chain(1, 0)
    chain(0, Z - 2)
    for s in range(1, Z - 1):
        chain(1, s)
    finish(0)
    finish(1)

    pre = dot(agg[...], weight[...])
    sigma = 1.0 / (1.0 + jnp.exp(-pre))
    dpre = (ngrad[...].astype(F32) * sigma * (1.0 + pre * (1.0 - sigma))).astype(BF)
    dpre_v[...] = dpre
    out[...] = (pre * sigma).astype(BF)

    def gsib_copy(h, owner):
        rows = tile_at(2 * owner + c)
        return remote(
            grads.at[h, rows, :], grads.at[h, rows, :], gsib_s.at[h, owner], gsib_r.at[h, owner],
            i, sibling,
        )

    def gup_copy(h, s):
        rows = tile_at(2 * jnp.maximum(z - s, 0) + c)
        return remote(
            grads.at[h, rows, :], grads.at[h, rows, :], gup_s.at[h, s], gup_r.at[h, s],
            i, 2 * above + c,
        )

    def gdn_copy(h, s):
        rows = tile_at(2 * jnp.minimum(z + s, Z - 1) + c)
        return remote(
            grads.at[h, rows, :], grads.at[h, rows, :], gdn_s.at[h, s], gdn_r.at[h, s],
            i, 2 * below + c,
        )

    for h in range(H):
        part = lax.dot_general(
            dpre_v[...],
            weight[h * W : (h + 1) * W, :],
            (((1,), (1,)), ((), ())),
            preferred_element_type=F32,
        )
        grads[h, tile_at(j), :] = part.astype(BF)
        send(gup_copy(h, 0), z < Z - 1)
        send(gdn_copy(h, 0), z > 0)
        send(gsib_copy(h, z))

    S1 = F // R
    groups = S1 // 16
    cg = C // groups
    width = F // cg

    def slab_at(index):
        return pl.ds(pl.multiple_of(index * S1, S1), S1)

    def piece_at(index):
        return (
            pl.ds(pl.multiple_of(index // cg * 16, 16), 16),
            pl.ds(pl.multiple_of(lax.rem(index, cg) * width, width), width),
        )

    def w1_copy(q):
        return remote(
            w1_send.at[q - 1], w1_recv.at[q - 1], w1_s.at[q - 1], w1_r.at[q - 1],
            lax.rem(i + q, R), j,
        )

    def w2_copy(q):
        return remote(
            w2_send.at[q - 1], w2_recv.at[q - 1], w2_s.at[q - 1], w2_r.at[q - 1],
            i, lax.rem(j + q, C),
        )

    def w3_copy(q, owner):
        r, k = piece_at(owner)
        return remote(
            wslab.at[r, k], wslab.at[r, k], w3_s.at[q - 1], w3_r.at[q - 1], i, lax.rem(j + q, C)
        )

    def w4_copy(q, owner):
        rows = slab_at(owner)
        return remote(
            wslab, wfull.at[rows, :], w4_s.at[q - 1], w4_r.at[q - 1], lax.rem(i + q, R), j
        )

    wterm[...] = (
        lax.dot_general(
            agg[...], dpre_v[...], (((0,), (0,)), ((), ())), preferred_element_type=F32
        )
        * scale
    )
    for q in range(1, R):
        w1_send[q - 1] = wterm[slab_at(lax.rem(i + q, R)), :].astype(BF)
        send(w1_copy(q))

    def gather(h, s):
        from_below = z - 1 - s >= 0
        from_above = z + 1 + s <= Z - 1

        @pl.when(from_below)
        def _():
            gup_copy(h, s).wait_recv()

        if s + 1 < Z - 1:
            send(gup_copy(h, s + 1), from_below & (z < Z - 1))
        send(gsib_copy(h, jnp.maximum(z - 1 - s, 0)), from_below)

        @pl.when(from_above)
        def _():
            gdn_copy(h, s).wait_recv()

        if s + 1 < Z - 1:
            send(gdn_copy(h, s + 1), from_above & (z > 0))
        send(gsib_copy(h, jnp.minimum(z + 1 + s, Z - 1)), from_above)

    def b_copy(h, q):
        return remote(
            b_send.at[h, q - 1], b_recv.at[h, q - 1], b_s.at[h, q - 1], b_r.at[h, q - 1],
            lax.rem(i + q, R), j,
        )

    def backward(h):
        for d in range(Z):
            gsib_copy(h, d).wait_recv()
        for q in range(1, R):
            b_send[h, q - 1] = dot(denseT[lax.rem(i + q, R)], grads[h]).astype(BF)
            send(b_copy(h, q))

    def total(h):
        acc = dot(denseT[i], grads[h])
        for q in range(1, R):
            b_copy(h, q).wait_recv()
            acc = acc + b_recv[h, q - 1].astype(F32)
        fgrad[:, h * W : (h + 1) * W] = acc.astype(BF)

    gather(0, 0)
    gather(1, 0)
    acc = wterm[slab_at(i), :]
    for q in range(1, R):
        w1_copy(q).wait_recv()
        acc = acc + w1_recv[q - 1].astype(F32)
    w1_sum[...] = acc
    for q in range(1, C):
        r, k = piece_at(lax.rem(j + q, C))
        w2_send[q - 1] = w1_sum[r, k].astype(BF)
        send(w2_copy(q))
    gather(0, 1)
    gather(1, 1)
    r, k = piece_at(j)
    acc = w1_sum[r, k]
    for q in range(1, C):
        w2_copy(q).wait_recv()
        acc = acc + w2_recv[q - 1].astype(F32)
    wslab[r, k] = acc.astype(BF)
    for q in range(1, C):
        send(w3_copy(q, j))
    for s in range(2, Z - 1):
        gather(0, s)
        gather(1, s)
    backward(0)
    for q in range(1, C):
        w3_copy(q, lax.rem(j - q + C, C)).wait_recv()
    backward(1)
    for q in range(1, R):
        send(w4_copy(q, i))
    wfull[slab_at(i), :] = wslab[...]
    total(0)
    total(1)
    for q in range(1, R):
        w4_copy(q, lax.rem(i - q + R, R)).wait_recv()
    wout[...] = wfull[...].astype(F32)

    for copy, cond in pending:
        if cond is None:
            copy.wait_send()
        else:
            pl.when(cond)(copy.wait_send)


def local(adj_tiles, tile_rows, tile_cols, tile_counts, features, weight, node_grad):
    R = lax.axis_size("row")
    C = lax.axis_size("col")
    Z = C // 2
    H = HALVES
    T, F = features.shape
    W = F // H
    slots = adj_tiles.shape[2]
    S1 = F // R
    width = F // (C // (S1 // 16))
    scale = float((T * R * C) ** -0.5)
    vmem = pltpu.VMEM
    dma = pltpu.SemaphoreType.DMA
    scratch = [
        vmem((slots + 1, T, T), BF),
        pltpu.SMEM((C * R,), jnp.int32),
        vmem((R, T, C * T), BF),
        vmem((H, R * T, W), BF),
        vmem((H, Z, T, W), BF),
        vmem((H, Z, T, W), BF),
        vmem((H, Z, T, W), BF),
        vmem((H, Z - 1, T, W), BF),
        vmem((H, Z - 1, T, W), BF),
        vmem((T, F), BF),
        vmem((T, F), BF),
        vmem((H, C * T, W), BF),
        vmem((H, R - 1, T, W), BF),
        vmem((H, R - 1, T, W), BF),
        vmem((F, F), F32),
        vmem((R - 1, S1, F), BF),
        vmem((R - 1, S1, F), BF),
        vmem((S1, F), F32),
        vmem((C - 1, 16, width), BF),
        vmem((C - 1, 16, width), BF),
        vmem((S1, F), BF),
        vmem((F, F), BF),
        dma(()),
    ]
    for shape in (
        (H, R - 1),
        (H, Z),
        (H, Z - 1),
        (H, Z - 1),
        (H, Z),
        (H, Z - 1),
        (H, Z - 1),
        (H, R - 1),
        (R - 1,),
        (C - 1,),
        (C - 1,),
        (R - 1,),
    ):
        scratch += [dma(shape), dma(shape)]
    whole = pl.BlockSpec(memory_space=pltpu.VMEM)
    scalars = pl.BlockSpec(memory_space=pltpu.SMEM)
    return pl.pallas_call(
        functools.partial(kernel, R, C, scale),
        out_shape=(
            jax.ShapeDtypeStruct((T, F), BF),
            jax.ShapeDtypeStruct((F, F), F32),
            jax.ShapeDtypeStruct((T, F), BF),
        ),
        in_specs=[scalars] * 3 + [pl.BlockSpec(memory_space=pl.ANY)] + [whole] * 3,
        out_specs=(whole, whole, whole),
        scratch_shapes=scratch,
        compiler_params=pltpu.CompilerParams(
            collective_id=0, has_side_effects=True, vmem_limit_bytes=60 * 1024 * 1024
        ),
        name="layer",
    )(tile_rows, tile_cols, tile_counts, adj_tiles, features, weight, node_grad)


def solution(mesh):
    in_specs = (
        P("row", "col", None, None, None),
        P("row", "col", None),
        P("row", "col", None),
        P("row", "col"),
        P(("col", "row"), None),
        P(),
        P(("row", "col"), None),
    )
    out_specs = (P(("row", "col"), None), P(), P(("col", "row"), None))
    return jax.shard_map(local, mesh=mesh, in_specs=in_specs, out_specs=out_specs, check_vma=False)
```

time: 350 us -> 97.5 us (0.28)
  waiting for transfers between devices: 254 us -> 0 us
  Pallas kernels: 0 us -> 91.4 us
  matrix products: 46.2 us -> 0 us
  local copies, waits for them, and re-layouts: 30.6 us -> 4.68 us
  between operations: 14.5 us -> 1.29 us
    psum x1 -> x0, waiting for transfers between devices: 101 us -> none  [local(): weight_grad = lax.psum(weight_term, ('row', 'col'))]
    reduce_scatter x2 -> x0, waiting for transfers between devices: 96.1 us -> none  [the longest x1 65.8 us: local(): lax.psum_scatter(partial_value.reshape(row_tiles * tile_size, feat_width)...]
    pallas_call x0 -> x1, Pallas kernels: none -> 91.4 us  [local(): pl.pallas_call(functools.partial(kernel, R, C, scale), out_shape=(jax.Sha...]
    all_gather x2 -> x0, waiting for transfers between devices: 56.9 us -> none  [the longest x1 30.6 us: local(): column_feats = lax.all_gather(features, 'row', axis=0, tiled=True)]
    dot_general x7 -> x0, matrix products: 46.2 us -> none  [the longest x2 27.3 us: add_block(): jnp.einsum('ds,saf->daf', placing, products, precision=lax.Precision.HIGH...]
    gather x10 -> x0, local copies, waits for them, and re-layouts: 17.3 us -> none  [the longest x2 7.18 us: add_block(): source_pieces = jnp.take(source, source_block, axis=0)]
    while x1 -> x0, local copies, waits for them, and re-layouts: 5.8 us -> none  [spread_tiles(): return lax.fori_loop(0, block_total, add_block, start_value)]
    broadcast_in_dim x2 -> x0, local copies, waits for them, and re-layouts: 4.02 us -> none  [spread_tiles(): start_value = jnp.zeros((dest_tiles, tile_size, feat_width), jnp.float32)]
  transfers between devices with their start and end apart: 5 -> 0, of which waited for: 5 -> 0; matrix products, arithmetic and copies ran while one was open for 10% -> 0% of each run, Pallas kernels for 0% -> 0%
where the time goes in v1:
time: 97.5 us; the launch traced here: 97.3 us
  Pallas kernels  91.4 us (94%)
  local copies, waits for them, and re-layouts  4.68 us (5%)
  between operations  1.29 us (1%)
    pallas_call x1, Pallas kernels, local(): pl.pallas_call(functools.partial(kernel, R, C, scale), out_shape=(jax.Sha...  91.4 us
    unnamed x5, local copies, waits for them, and re-layouts  4.68 us

profile of v1, /device:TPU:0, one launch (start us, length us, event | category | flops | bytes accessed | tf_op | source)
XLA Modules:
  0.0 97.3 jit_solution(10182343326436300479)
XLA Ops:
  1.3 91.4 %layer.1 = (bf16[256,512]{1,0:T(8,128)(2,1)}, f32[512,512]{1,0:T(8,128)}, bf16[256,512]{1,0:T(8,128)(2,1)}) custom-call(s32[1,1,20]{2,1,0:T(1,128)} %rows_s.1, s32[1,1,20]{2,1,0:T(1,128)} %cols_s.1, s32[1,1]{1,0:T(1,128)S(6)} %copy.13.count_s, bf16[1,1,20,256,256]{4,3,2,1,0:T(8,128)(2,1)} %adj_hbm.1, bf16[256,512]{1,0:T(8,128)(2,1)} %feat.1, ...), custom_call_target="tpu_custom_call" | custom-call | tf_op jit(solution)/shard_map/layer/pallas_call | solution.py:474
  92.6 0.0 copy-start
  92.7 1.7 %copy.14 = bf16[256,512]{1,0:T(8,128)(2,1)} copy(bf16[256,512]{1,0:T(8,128)(2,1)} %get-tuple-element.6) | data formatting | bytes 524288
  94.4 2.3 %copy.15 = f32[512,512]{1,0:T(8,128)} copy(f32[512,512]{1,0:T(8,128)} %get-tuple-element.7) | data formatting | bytes 2097152
  96.6 0.0 copy-done
  96.6 0.7 copy.16
Async XLA Ops:
  92.6 4.0 %copy-start = (bf16[256,512]{1,0:T(8,128)(2,1)S(1)}, bf16[256,512]{1,0:T(8,128)(2,1)}, u32[]{:S(2)}) copy-start(bf16[256,512]{1,0:T(8,128)(2,1)} %get-tuple-element.8) | copy-start | bytes 786436

commit v2 on v1

--- a/solution.py
+++ b/solution.py
@@ -28,11 +28,10 @@
     weight,
     ngrad,
     out,
-    wout,
+    wfull,
     fgrad,
     adj,
     place,
-    denseT,
     feats,
     chip,
     sib_send,
@@ -45,13 +44,15 @@
     b_send,
     b_recv,
     wterm,
+    w0_send,
+    w0_recv,
+    w_pair,
     w1_send,
     w1_recv,
     w1_sum,
     w2_send,
     w2_recv,
     wslab,
-    wfull,
     adj_sem,
     f_s,
     f_r,
@@ -69,6 +70,8 @@
     gdn_r,
     b_s,
     b_r,
+    w0_s,
+    w0_r,
     w1_s,
     w1_r,
     w2_s,
@@ -77,6 +80,8 @@
     w3_r,
     w4_s,
     w4_r,
+    w5_s,
+    w5_r,
 ):
     H = HALVES
     Z = C // 2
@@ -151,7 +156,6 @@
                 hit = (rows_s[0, 0, t] == r) & (cols_s[0, 0, t] == k) & (t < count)
                 found = jnp.where(hit, jnp.int32(t), found)
             place[r * R + k] = found
-            denseT[k, :, tile_at(r)] = adj[found].T
         return carry
 
     lax.fori_loop(0, C, fill, 0)
@@ -249,48 +253,53 @@
     sigma = 1.0 / (1.0 + jnp.exp(-pre))
     dpre = (ngrad[...].astype(F32) * sigma * (1.0 + pre * (1.0 - sigma))).astype(BF)
     dpre_v[...] = dpre
-    out[...] = (pre * sigma).astype(BF)
 
     def gsib_copy(h, owner):
-        rows = tile_at(2 * owner + c)
-        return remote(
-            grads.at[h, rows, :], grads.at[h, rows, :], gsib_s.at[h, owner], gsib_r.at[h, owner],
+        r = 2 * owner + c
+        return remote(
+            grads.at[h, r], grads.at[h, r], gsib_s.at[h, owner], gsib_r.at[h, owner],
             i, sibling,
         )
 
     def gup_copy(h, s):
-        rows = tile_at(2 * jnp.maximum(z - s, 0) + c)
-        return remote(
-            grads.at[h, rows, :], grads.at[h, rows, :], gup_s.at[h, s], gup_r.at[h, s],
+        r = 2 * jnp.maximum(z - s, 0) + c
+        return remote(
+            grads.at[h, r], grads.at[h, r], gup_s.at[h, s], gup_r.at[h, s],
             i, 2 * above + c,
         )
 
     def gdn_copy(h, s):
-        rows = tile_at(2 * jnp.minimum(z + s, Z - 1) + c)
-        return remote(
-            grads.at[h, rows, :], grads.at[h, rows, :], gdn_s.at[h, s], gdn_r.at[h, s],
+        r = 2 * jnp.minimum(z + s, Z - 1) + c
+        return remote(
+            grads.at[h, r], grads.at[h, r], gdn_s.at[h, s], gdn_r.at[h, s],
             i, 2 * below + c,
         )
 
     for h in range(H):
         part = lax.dot_general(
+            weight[h * W : (h + 1) * W, :],
             dpre_v[...],
-            weight[h * W : (h + 1) * W, :],
             (((1,), (1,)), ((), ())),
             preferred_element_type=F32,
         )
-        grads[h, tile_at(j), :] = part.astype(BF)
+        grads[h, j] = part.astype(BF)
         send(gup_copy(h, 0), z < Z - 1)
         send(gdn_copy(h, 0), z > 0)
         send(gsib_copy(h, z))
 
-    S1 = F // R
+    out[...] = (pre * sigma).astype(BF)
+
+    half = F // 2
+    S1 = half // R
     groups = S1 // 16
-    cg = C // groups
+    cg = Z // groups
     width = F // cg
 
     def slab_at(index):
         return pl.ds(pl.multiple_of(index * S1, S1), S1)
+
+    def half_at(index):
+        return pl.ds(pl.multiple_of(index * half, half), half)
 
     def piece_at(index):
         return (
@@ -298,6 +307,8 @@
             pl.ds(pl.multiple_of(lax.rem(index, cg) * width, width), width),
         )
 
+    w0_copy = remote(w0_send, w0_recv, w0_s, w0_r, i, sibling)
+
     def w1_copy(q):
         return remote(
             w1_send.at[q - 1], w1_recv.at[q - 1], w1_s.at[q - 1], w1_r.at[q - 1],
@@ -307,20 +318,25 @@
     def w2_copy(q):
         return remote(
             w2_send.at[q - 1], w2_recv.at[q - 1], w2_s.at[q - 1], w2_r.at[q - 1],
-            i, lax.rem(j + q, C),
+            i, 2 * lax.rem(z + q, Z) + c,
         )
 
     def w3_copy(q, owner):
         r, k = piece_at(owner)
         return remote(
-            wslab.at[r, k], wslab.at[r, k], w3_s.at[q - 1], w3_r.at[q - 1], i, lax.rem(j + q, C)
+            wslab.at[r, k], wslab.at[r, k], w3_s.at[q - 1], w3_r.at[q - 1],
+            i, 2 * lax.rem(z + q, Z) + c,
         )
 
     def w4_copy(q, owner):
-        rows = slab_at(owner)
+        rows = slab_at(c * R + owner)
         return remote(
             wslab, wfull.at[rows, :], w4_s.at[q - 1], w4_r.at[q - 1], lax.rem(i + q, R), j
         )
+
+    def w5_copy(core):
+        rows = half_at(core)
+        return remote(wfull.at[rows, :], wfull.at[rows, :], w5_s, w5_r, i, sibling)
 
     wterm[...] = (
         lax.dot_general(
@@ -328,9 +344,48 @@
         )
         * scale
     )
-    for q in range(1, R):
-        w1_send[q - 1] = wterm[slab_at(lax.rem(i + q, R)), :].astype(BF)
-        send(w1_copy(q))
+    w0_send[...] = wterm[half_at(1 - c), :].astype(BF)
+    send(w0_copy)
+
+    def sum_pair():
+        w0_copy.wait_recv()
+        w_pair[...] = wterm[half_at(c), :] + w0_recv[...].astype(F32)
+        for q in range(1, R):
+            w1_send[q - 1] = w_pair[slab_at(lax.rem(i + q, R)), :].astype(BF)
+            send(w1_copy(q))
+
+    def sum_row():
+        acc = w_pair[slab_at(i), :]
+        for q in range(1, R):
+            w1_copy(q).wait_recv()
+            acc = acc + w1_recv[q - 1].astype(F32)
+        w1_sum[...] = acc
+        for q in range(1, Z):
+            r, k = piece_at(lax.rem(z + q, Z))
+            w2_send[q - 1] = w1_sum[r, k].astype(BF)
+            send(w2_copy(q))
+
+    def sum_chain():
+        r, k = piece_at(z)
+        acc = w1_sum[r, k]
+        for q in range(1, Z):
+            w2_copy(q).wait_recv()
+            acc = acc + w2_recv[q - 1].astype(F32)
+        wslab[r, k] = acc.astype(BF)
+        for q in range(1, Z):
+            send(w3_copy(q, z))
+
+    def share_row():
+        for q in range(1, Z):
+            w3_copy(q, lax.rem(z - q + Z, Z)).wait_recv()
+        for q in range(1, R):
+            send(w4_copy(q, i))
+        wfull[slab_at(c * R + i), :] = wslab[...]
+
+    def share_pair():
+        for q in range(1, R):
+            w4_copy(q, lax.rem(i - q + R, R)).wait_recv()
+        send(w5_copy(c))
 
     def gather(h, s):
         from_below = z - 1 - s >= 0
@@ -358,62 +413,55 @@
             lax.rem(i + q, R), j,
         )
 
+    def cell_cols(h, k):
+        acc = dot(grads[h, 0], adj[place[k]])
+        for r in range(1, C):
+            acc = acc + dot(grads[h, r], adj[place[r * R + k]])
+        return acc
+
     def backward(h):
         for d in range(Z):
             gsib_copy(h, d).wait_recv()
         for q in range(1, R):
-            b_send[h, q - 1] = dot(denseT[lax.rem(i + q, R)], grads[h]).astype(BF)
+            b_send[h, q - 1] = cell_cols(h, lax.rem(i + q, R)).astype(BF)
             send(b_copy(h, q))
 
     def total(h):
-        acc = dot(denseT[i], grads[h])
+        acc = cell_cols(h, i)
         for q in range(1, R):
             b_copy(h, q).wait_recv()
             acc = acc + b_recv[h, q - 1].astype(F32)
-        fgrad[:, h * W : (h + 1) * W] = acc.astype(BF)
+        fgrad[:, h * W : (h + 1) * W] = acc.T.astype(BF)
 
     gather(0, 0)
+    sum_pair()
+    gather(0, 1)
     gather(1, 0)
-    acc = wterm[slab_at(i), :]
-    for q in range(1, R):
-        w1_copy(q).wait_recv()
-        acc = acc + w1_recv[q - 1].astype(F32)
-    w1_sum[...] = acc
-    for q in range(1, C):
-        r, k = piece_at(lax.rem(j + q, C))
-        w2_send[q - 1] = w1_sum[r, k].astype(BF)
-        send(w2_copy(q))
-    gather(0, 1)
-    gather(1, 1)
-    r, k = piece_at(j)
-    acc = w1_sum[r, k]
-    for q in range(1, C):
-        w2_copy(q).wait_recv()
-        acc = acc + w2_recv[q - 1].astype(F32)
-    wslab[r, k] = acc.astype(BF)
-    for q in range(1, C):
-        send(w3_copy(q, j))
+    sum_row()
     for s in range(2, Z - 1):
         gather(0, s)
-        gather(1, s)
+        gather(1, s - 1)
     backward(0)
-    for q in range(1, C):
-        w3_copy(q, lax.rem(j - q + C, C)).wait_recv()
+    sum_chain()
+    gather(1, Z - 2)
+    share_row()
     backward(1)
-    for q in range(1, R):
-        send(w4_copy(q, i))
-    wfull[slab_at(i), :] = wslab[...]
     total(0)
+    share_pair()
     total(1)
-    for q in range(1, R):
-        w4_copy(q, lax.rem(i - q + R, R)).wait_recv()
-    wout[...] = wfull[...].astype(F32)
+    w5_copy(1 - c).wait_recv()
 
     for copy, cond in pending:
         if cond is None:
             copy.wait_send()
         else:
             pl.when(cond)(copy.wait_send)
+
+
+def hand_over(node_in, weight_in, feature_in, node_out, weight_out, feature_out):
+    node_out[...] = node_in[...]
+    weight_out[...] = weight_in[...].astype(F32)
+    feature_out[...] = feature_in[...]
 
 
 def local(adj_tiles, tile_rows, tile_cols, tile_counts, features, weight, node_grad):
@@ -424,15 +472,14 @@
     T, F = features.shape
     W = F // H
     slots = adj_tiles.shape[2]
-    S1 = F // R
-    width = F // (C // (S1 // 16))
+    S1 = F // 2 // R
+    width = F // (Z // (S1 // 16))
     scale = float((T * R * C) ** -0.5)
     vmem = pltpu.VMEM
     dma = pltpu.SemaphoreType.DMA
     scratch = [
         vmem((slots + 1, T, T), BF),
         pltpu.SMEM((C * R,), jnp.int32),
-        vmem((R, T, C * T), BF),
         vmem((H, R * T, W), BF),
         vmem((H, Z, T, W), BF),
         vmem((H, Z, T, W), BF),
@@ -441,17 +488,19 @@
         vmem((H, Z - 1, T, W), BF),
         vmem((T, F), BF),
         vmem((T, F), BF),
-        vmem((H, C * T, W), BF),
-        vmem((H, R - 1, T, W), BF),
-        vmem((H, R - 1, T, W), BF),
+        vmem((H, C, W, T), BF),
+        vmem((H, R - 1, W, T), BF),
+        vmem((H, R - 1, W, T), BF),
         vmem((F, F), F32),
+        vmem((F // 2, F), BF),
+        vmem((F // 2, F), BF),
+        vmem((F // 2, F), F32),
         vmem((R - 1, S1, F), BF),
         vmem((R - 1, S1, F), BF),
         vmem((S1, F), F32),
-        vmem((C - 1, 16, width), BF),
-        vmem((C - 1, 16, width), BF),
+        vmem((Z - 1, 16, width), BF),
+        vmem((Z - 1, 16, width), BF),
         vmem((S1, F), BF),
-        vmem((F, F), BF),
         dma(()),
     ]
     for shape in (
@@ -463,19 +512,21 @@
         (H, Z - 1),
         (H, Z - 1),
         (H, R - 1),
+        (),
         (R - 1,),
-        (C - 1,),
-        (C - 1,),
+        (Z - 1,),
+        (Z - 1,),
         (R - 1,),
+        (),
     ):
         scratch += [dma(shape), dma(shape)]
     whole = pl.BlockSpec(memory_space=pltpu.VMEM)
     scalars = pl.BlockSpec(memory_space=pltpu.SMEM)
-    return pl.pallas_call(
+    node_out, weight_grad, feature_grad = pl.pallas_call(
         functools.partial(kernel, R, C, scale),
         out_shape=(
             jax.ShapeDtypeStruct((T, F), BF),
-            jax.ShapeDtypeStruct((F, F), F32),
+            jax.ShapeDtypeStruct((F, F), BF),
             jax.ShapeDtypeStruct((T, F), BF),
         ),
         in_specs=[scalars] * 3 + [pl.BlockSpec(memory_space=pl.ANY)] + [whole] * 3,
@@ -486,6 +537,17 @@
         ),
         name="layer",
     )(tile_rows, tile_cols, tile_counts, adj_tiles, features, weight, node_grad)
+    return pl.pallas_call(
+        hand_over,
+        out_shape=(
+            jax.ShapeDtypeStruct((T, F), BF),
+            jax.ShapeDtypeStruct((F, F), F32),
+            jax.ShapeDtypeStruct((T, F), BF),
+        ),
+        in_specs=[whole] * 3,
+        out_specs=(whole, whole, whole),
+        name="hand_over",
+    )(node_out, weight_grad, feature_grad)
 
 
 def solution(mesh):

time: 97.5 us -> 89 us (0.913)
  local copies, waits for them, and re-layouts: 4.68 us -> 0 us
  Pallas kernels: 91.4 us -> 87.5 us
    pallas_call x1, Pallas kernels: 91.4 us -> 85.1 us  [local(): pl.pallas_call(functools.partial(kernel, R, C, scale), out_shape=(jax.Sha...]
    unnamed x5 -> x0, local copies, waits for them, and re-layouts: 4.68 us -> none
    pallas_call x0 -> x1, Pallas kernels: none -> 2.41 us  [local(): pl.pallas_call(hand_over, out_shape=(jax.ShapeDtypeStruct((T, F), BF), ja...]
where the time goes in v2:
time: 89 us; the launch traced here: 88.8 us
  Pallas kernels  87.5 us (98%)
  between operations  1.29 us (1%)
    pallas_call x1, Pallas kernels, local(): pl.pallas_call(functools.partial(kernel, R, C, scale), out_shape=(jax.Sha...  85.1 us
    pallas_call x1, Pallas kernels, local(): pl.pallas_call(hand_over, out_shape=(jax.ShapeDtypeStruct((T, F), BF), ja...  2.41 us

profile of v2, /device:TPU:0, one launch (start us, length us, event | category | flops | bytes accessed | tf_op | source)
XLA Modules:
  0.0 88.8 jit_solution(6167130072405794886)
XLA Ops:
  1.3 85.1 %layer.1 = (bf16[256,512]{1,0:T(8,128)(2,1)}, bf16[512,512]{1,0:T(8,128)(2,1)}, bf16[256,512]{1,0:T(8,128)(2,1)}) custom-call(s32[1,1,20]{2,1,0:T(1,128)} %rows_s.1, s32[1,1,20]{2,1,0:T(1,128)} %cols_s.1, s32[1,1]{1,0:T(1,128)S(6)} %copy.10.count_s, bf16[1,1,20,256,256]{4,3,2,1,0:T(8,128)(2,1)} %adj_hbm.1, bf16[256,512]{1,0:T(8,128)(2,1)} %feat.1, ...), custom_call_target="tpu_custom_call" | custom-call | tf_op jit(solution)/shard_map/layer/pallas_call | solution.py:525
  86.4 2.4 %hand_over.1 = (bf16[256,512]{1,0:T(8,128)(2,1)}, f32[512,512]{1,0:T(8,128)}, bf16[256,512]{1,0:T(8,128)(2,1)}) custom-call(bf16[256,512]{1,0:T(8,128)(2,1)} %get-tuple-element.6.node_in, bf16[512,512]{1,0:T(8,128)(2,1)} %get-tuple-element.7.weight_in, bf16[256,512]{1,0:T(8,128)(2,1)} %get-tuple-element.8.feature_in), custom_call_target="tpu_custom_call" | custom-call | tf_op jit(solution)/shard_map/hand_over/pallas_call | solution.py:540

commit v3 on v2

--- a/solution.py
+++ b/solution.py
@@ -9,7 +9,7 @@
 
 BF = jnp.bfloat16
 F32 = jnp.float32
-HALVES = 2
+CHUNKS = 4
 
 
 def dot(a, b):
@@ -31,7 +31,7 @@
     wfull,
     fgrad,
     adj,
-    place,
+    dense,
     feats,
     chip,
     sib_send,
@@ -83,7 +83,7 @@
     w5_s,
     w5_r,
 ):
-    H = HALVES
+    H = CHUNKS
     Z = C // 2
     T, F = feat.shape
     W = F // H
@@ -120,11 +120,17 @@
         pl.semaphore_signal(
             barrier, inc=1, device_id=(lax.rem(i + q, R), j), device_id_type=pl.DeviceIdType.MESH
         )
-    for q in range(1, C):
+    for q in range(1, Z):
         pl.semaphore_signal(
-            barrier, inc=1, device_id=(i, lax.rem(j + q, C)), device_id_type=pl.DeviceIdType.MESH
-        )
-    pl.semaphore_wait(barrier, R + C - 2)
+            barrier,
+            inc=1,
+            device_id=(i, 2 * lax.rem(z + q, Z) + c),
+            device_id_type=pl.DeviceIdType.MESH,
+        )
+    pl.semaphore_signal(
+        barrier, inc=1, device_id=(i, sibling), device_id_type=pl.DeviceIdType.MESH
+    )
+    pl.semaphore_wait(barrier, R + Z - 1)
 
     def tile_at(index):
         return pl.ds(pl.multiple_of(index * T, T), T)
@@ -155,50 +161,37 @@
             for t in range(slots):
                 hit = (rows_s[0, 0, t] == r) & (cols_s[0, 0, t] == k) & (t < count)
                 found = jnp.where(hit, jnp.int32(t), found)
-            place[r * R + k] = found
+            dense[tile_at(lax.rem(r, 2) * Z + r // 2), k * T : (k + 1) * T] = adj[found]
         return carry
 
     lax.fori_loop(0, C, fill, 0)
 
-    order = []
-    for s in range((Z + 1) // 2):
-        order.append(Z - 1 - s)
-        if s != Z - 1 - s:
-            order.append(s)
-
-    def sib_copy(h, d):
-        return remote(
-            sib_send.at[h, d], sib_recv.at[h, d], sib_s.at[h, d], sib_r.at[h, d], i, sibling
-        )
-
-    def cell_rows(h, r):
-        acc = dot(adj[place[r * R]], feats[h, :T, :])
-        for k in range(1, R):
-            acc = acc + dot(adj[place[r * R + k]], feats[h, k * T : (k + 1) * T, :])
-        return acc
+    def core_rows(core):
+        return pl.ds(pl.multiple_of(core * Z * T, Z * T), Z * T)
+
+    def sib_copy(h):
+        return remote(sib_send.at[h], sib_recv.at[h], sib_s.at[h], sib_r.at[h], i, sibling)
 
     def forward(h):
         for q in range(1, R):
             feat_copy(h, q).wait_recv()
-        for d in order:
-            sib_send[h, d] = cell_rows(h, 2 * d + 1 - c).astype(BF)
-            send(sib_copy(h, d))
-        for d in order:
-            part = cell_rows(h, 2 * d + c)
-            sib_copy(h, d).wait_recv()
-            chip[h, d] = (part + sib_recv[h, d].astype(F32)).astype(BF)
+        sib_send[h] = dot(dense[core_rows(1 - c), :], feats[h]).astype(BF)
+        send(sib_copy(h))
+        part = dot(dense[core_rows(c), :], feats[h])
+        sib_copy(h).wait_recv()
+        chip[h] = (part + sib_recv[h].astype(F32)).astype(BF)
 
     above = jnp.minimum(z + 1, Z - 1)
     below = jnp.maximum(z - 1, 0)
 
     def up_copy(h, s):
         return remote(
-            chip.at[h, Z - 1 - s], up_recv.at[h, s], up_s.at[h, s], up_r.at[h, s], i, 2 * above + c
+            chip.at[h, pl.ds((Z - 1 - s) * T, T)], up_recv.at[h, s], up_s.at[h, s], up_r.at[h, s], i, 2 * above + c
         )
 
     def dn_copy(h, s):
         return remote(
-            chip.at[h, s], dn_recv.at[h, s], dn_s.at[h, s], dn_r.at[h, s], i, 2 * below + c
+            chip.at[h, pl.ds(s * T, T)], dn_recv.at[h, s], dn_s.at[h, s], dn_r.at[h, s], i, 2 * below + c
         )
 
     def chain(h, s):
@@ -207,14 +200,14 @@
         @pl.when((z > 0) & (z < d))
         def _():
             up_copy(h, s).wait_recv()
-            chip[h, d] = (chip[h, d].astype(F32) + up_recv[h, s].astype(F32)).astype(BF)
+            chip[h, d * T : (d + 1) * T] = (chip[h, d * T : (d + 1) * T].astype(F32) + up_recv[h, s].astype(F32)).astype(BF)
 
         send(up_copy(h, s), z < d)
 
         @pl.when((z < Z - 1) & (z > s))
         def _():
             dn_copy(h, s).wait_recv()
-            chip[h, s] = (chip[h, s].astype(F32) + dn_recv[h, s].astype(F32)).astype(BF)
+            chip[h, s * T : (s + 1) * T] = (chip[h, s * T : (s + 1) * T].astype(F32) + dn_recv[h, s].astype(F32)).astype(BF)
 
         send(dn_copy(h, s), z > s)
 
@@ -224,30 +217,29 @@
         @pl.when(z == 0)
         def _():
             dn_copy(h, z).wait_recv()
-            agg[:, cols] = (chip[h, z].astype(F32) + dn_recv[h, z].astype(F32)).astype(BF)
+            agg[:, cols] = (chip[h, tile_at(z)].astype(F32) + dn_recv[h, z].astype(F32)).astype(BF)
 
         @pl.when(z == Z - 1)
         def _():
             up_copy(h, Z - 1 - z).wait_recv()
-            agg[:, cols] = (chip[h, z].astype(F32) + up_recv[h, Z - 1 - z].astype(F32)).astype(BF)
+            agg[:, cols] = (chip[h, tile_at(z)].astype(F32) + up_recv[h, Z - 1 - z].astype(F32)).astype(BF)
 
         @pl.when((z > 0) & (z < Z - 1))
         def _():
             up_copy(h, Z - 1 - z).wait_recv()
             dn_copy(h, z).wait_recv()
             both = up_recv[h, Z - 1 - z].astype(F32) + dn_recv[h, z].astype(F32)
-            agg[:, cols] = (chip[h, z].astype(F32) + both).astype(BF)
-
-    forward(0)
-    for s in range(Z - 2):
-        chain(0, s)
-    forward(1)
-    chain(1, 0)
-    chain(0, Z - 2)
-    for s in range(1, Z - 1):
-        chain(1, s)
-    finish(0)
-    finish(1)
+            agg[:, cols] = (chip[h, tile_at(z)].astype(F32) + both).astype(BF)
+
+    for wave in range(H + Z - 2):
+        for s in range(Z - 2, 0, -1):
+            if 0 <= wave - s < H:
+                chain(wave - s, s)
+        if wave < H:
+            forward(wave)
+            chain(wave, 0)
+    for h in range(H):
+        finish(h)
 
     pre = dot(agg[...], weight[...])
     sigma = 1.0 / (1.0 + jnp.exp(-pre))
@@ -255,38 +247,39 @@
     dpre_v[...] = dpre
 
     def gsib_copy(h, owner):
-        r = 2 * owner + c
-        return remote(
-            grads.at[h, r], grads.at[h, r], gsib_s.at[h, owner], gsib_r.at[h, owner],
+        r = c * Z + owner
+        return remote(
+            grads.at[h, :, tile_at(r)], grads.at[h, :, tile_at(r)], gsib_s.at[h, owner], gsib_r.at[h, owner],
             i, sibling,
         )
 
     def gup_copy(h, s):
-        r = 2 * jnp.maximum(z - s, 0) + c
-        return remote(
-            grads.at[h, r], grads.at[h, r], gup_s.at[h, s], gup_r.at[h, s],
+        r = c * Z + jnp.maximum(z - s, 0)
+        return remote(
+            grads.at[h, :, tile_at(r)], grads.at[h, :, tile_at(r)], gup_s.at[h, s], gup_r.at[h, s],
             i, 2 * above + c,
         )
 
     def gdn_copy(h, s):
-        r = 2 * jnp.minimum(z + s, Z - 1) + c
-        return remote(
-            grads.at[h, r], grads.at[h, r], gdn_s.at[h, s], gdn_r.at[h, s],
+        r = c * Z + jnp.minimum(z + s, Z - 1)
+        return remote(
+            grads.at[h, :, tile_at(r)], grads.at[h, :, tile_at(r)], gdn_s.at[h, s], gdn_r.at[h, s],
             i, 2 * below + c,
         )
 
+    turned = lax.dot_general(
+        weight[...], dpre_v[...], (((1,), (1,)), ((), ())), preferred_element_type=F32
+    ).astype(BF)
     for h in range(H):
-        part = lax.dot_general(
-            weight[h * W : (h + 1) * W, :],
-            dpre_v[...],
-            (((1,), (1,)), ((), ())),
-            preferred_element_type=F32,
-        )
-        grads[h, j] = part.astype(BF)
+        grads[h, :, tile_at(c * Z + z)] = turned[h * W : (h + 1) * W, :]
+
+    def give(h):
         send(gup_copy(h, 0), z < Z - 1)
         send(gdn_copy(h, 0), z > 0)
         send(gsib_copy(h, z))
 
+    give(0)
+    give(1)
     out[...] = (pre * sigma).astype(BF)
 
     half = F // 2
@@ -414,10 +407,7 @@
         )
 
     def cell_cols(h, k):
-        acc = dot(grads[h, 0], adj[place[k]])
-        for r in range(1, C):
-            acc = acc + dot(grads[h, r], adj[place[r * R + k]])
-        return acc
+        return dot(grads[h], dense[:, tile_at(k)])
 
     def backward(h):
         for d in range(Z):
@@ -433,22 +423,28 @@
             acc = acc + b_recv[h, q - 1].astype(F32)
         fgrad[:, h * W : (h + 1) * W] = acc.T.astype(BF)
 
-    gather(0, 0)
-    sum_pair()
-    gather(0, 1)
-    gather(1, 0)
-    sum_row()
-    for s in range(2, Z - 1):
-        gather(0, s)
-        gather(1, s - 1)
-    backward(0)
-    sum_chain()
-    gather(1, Z - 2)
-    share_row()
-    backward(1)
-    total(0)
-    share_pair()
-    total(1)
+    for wave in range(H + Z - 2):
+        for s in range(Z - 2, -1, -1):
+            if 0 <= wave - s < H:
+                gather(wave - s, s)
+        if wave + 2 < H:
+            give(wave + 2)
+        if wave == 0:
+            sum_pair()
+        if wave == 1:
+            sum_row()
+        h = wave - (Z - 2)
+        if h >= 0:
+            backward(h)
+            if h == 0:
+                sum_chain()
+            if h == 1:
+                share_row()
+            if h == 2:
+                share_pair()
+            if h >= 1:
+                total(h - 1)
+    total(H - 1)
     w5_copy(1 - c).wait_recv()
 
     for copy, cond in pending:
@@ -468,7 +464,7 @@
     R = lax.axis_size("row")
     C = lax.axis_size("col")
     Z = C // 2
-    H = HALVES
+    H = CHUNKS
     T, F = features.shape
     W = F // H
     slots = adj_tiles.shape[2]
@@ -479,16 +475,16 @@
     dma = pltpu.SemaphoreType.DMA
     scratch = [
         vmem((slots + 1, T, T), BF),
-        pltpu.SMEM((C * R,), jnp.int32),
+        vmem((C * T, R * T), BF),
         vmem((H, R * T, W), BF),
-        vmem((H, Z, T, W), BF),
-        vmem((H, Z, T, W), BF),
-        vmem((H, Z, T, W), BF),
+        vmem((H, Z * T, W), BF),
+        vmem((H, Z * T, W), BF),
+        vmem((H, Z * T, W), BF),
         vmem((H, Z - 1, T, W), BF),
         vmem((H, Z - 1, T, W), BF),
         vmem((T, F), BF),
         vmem((T, F), BF),
-        vmem((H, C, W, T), BF),
+        vmem((H, W, C * T), BF),
         vmem((H, R - 1, W, T), BF),
         vmem((H, R - 1, W, T), BF),
         vmem((F, F), F32),
@@ -505,7 +501,7 @@
     ]
     for shape in (
         (H, R - 1),
-        (H, Z),
+        (H,),
         (H, Z - 1),
         (H, Z - 1),
         (H, Z),

time: 89 us -> 101 us (1.13)
  Pallas kernels: 87.5 us -> 99.6 us
    pallas_call x1, Pallas kernels: 85.1 us -> 97.2 us  [local(): pl.pallas_call(functools.partial(kernel, R, C, scale), out_shape=(jax.Sha...]
where the time goes in v3:
time: 101 us
  Pallas kernels  99.6 us (99%)
  between operations  1.29 us (1%)
    pallas_call x1, Pallas kernels, local(): pl.pallas_call(functools.partial(kernel, R, C, scale), out_shape=(jax.Sha...  97.2 us
    pallas_call x1, Pallas kernels, local(): pl.pallas_call(hand_over, out_shape=(jax.ShapeDtypeStruct((T, F), BF), ja...  2.41 us

profile of v3, /device:TPU:0, one launch (start us, length us, event | category | flops | bytes accessed | tf_op | source)
XLA Modules:
  0.0 100.9 jit_solution(582130090162119122)
XLA Ops:
  1.3 97.2 %layer.1 = (bf16[256,512]{1,0:T(8,128)(2,1)}, bf16[512,512]{1,0:T(8,128)(2,1)}, bf16[256,512]{1,0:T(8,128)(2,1)}) custom-call(s32[1,1,20]{2,1,0:T(1,128)} %rows_s.1, s32[1,1,20]{2,1,0:T(1,128)} %cols_s.1, s32[1,1]{1,0:T(1,128)S(6)} %copy.10.count_s, bf16[1,1,20,256,256]{4,3,2,1,0:T(8,128)(2,1)} %adj_hbm.1, bf16[256,512]{1,0:T(8,128)(2,1)} %feat.1, ...), custom_call_target="tpu_custom_call" | custom-call | tf_op jit(solution)/shard_map/layer/pallas_call | solution.py:521
  98.5 2.4 %hand_over.1 = (bf16[256,512]{1,0:T(8,128)(2,1)}, f32[512,512]{1,0:T(8,128)}, bf16[256,512]{1,0:T(8,128)(2,1)}) custom-call(bf16[256,512]{1,0:T(8,128)(2,1)} %get-tuple-element.6.node_in, bf16[512,512]{1,0:T(8,128)(2,1)} %get-tuple-element.7.weight_in, bf16[256,512]{1,0:T(8,128)(2,1)} %get-tuple-element.8.feature_in), custom_call_target="tpu_custom_call" | custom-call | tf_op jit(solution)/shard_map/hand_over/pallas_call | solution.py:536

commit v4 on v3

--- a/solution.py
+++ b/solution.py
@@ -9,7 +9,7 @@
 
 BF = jnp.bfloat16
 F32 = jnp.float32
-CHUNKS = 4
+CHUNKS = 2
 
 
 def dot(a, b):
@@ -41,6 +41,8 @@
     agg,
     dpre_v,
     grads,
+    wide,
+    b_own,
     b_send,
     b_recv,
     wterm,
@@ -115,6 +117,11 @@
     adj_copy = pltpu.make_async_copy(adj_hbm.at[0, 0], adj.at[pl.ds(0, slots)], adj_sem)
     adj_copy.start()
 
+    def tile_at(index):
+        return pl.ds(pl.multiple_of(index * T, T), T)
+
+    for h in range(H):
+        feats[h, tile_at(i), :] = feat[:, pl.ds(h * W, W)]
     barrier = pltpu.get_barrier_semaphore()
     for q in range(1, R):
         pl.semaphore_signal(
@@ -132,12 +139,9 @@
     )
     pl.semaphore_wait(barrier, R + Z - 1)
 
-    def tile_at(index):
-        return pl.ds(pl.multiple_of(index * T, T), T)
-
     def feat_copy(h, q):
         return remote(
-            feat.at[:, pl.ds(h * W, W)],
+            feats.at[h, tile_at(i), :],
             feats.at[h, tile_at(i), :],
             f_s.at[h, q - 1],
             f_r.at[h, q - 1],
@@ -148,8 +152,6 @@
     for h in range(H):
         for q in range(1, R):
             send(feat_copy(h, q))
-    for h in range(H):
-        feats[h, tile_at(i), :] = feat[:, pl.ds(h * W, W)]
 
     adj[slots] = jnp.zeros((T, T), BF)
     adj_copy.wait()
@@ -166,8 +168,10 @@
 
     lax.fori_loop(0, C, fill, 0)
 
-    def core_rows(core):
-        return pl.ds(pl.multiple_of(core * Z * T, Z * T), Z * T)
+    step = min(Z, 4) * T
+
+    def core_rows(core, first):
+        return pl.ds(pl.multiple_of(core * Z * T + first, step), step)
 
     def sib_copy(h):
         return remote(sib_send.at[h], sib_recv.at[h], sib_s.at[h], sib_r.at[h], i, sibling)
@@ -175,11 +179,16 @@
     def forward(h):
         for q in range(1, R):
             feat_copy(h, q).wait_recv()
-        sib_send[h] = dot(dense[core_rows(1 - c), :], feats[h]).astype(BF)
+        for first in range(0, Z * T, step):
+            part = dot(dense[core_rows(1 - c, first), :], feats[h])
+            sib_send[h, first : first + step] = part.astype(BF)
         send(sib_copy(h))
-        part = dot(dense[core_rows(c), :], feats[h])
-        sib_copy(h).wait_recv()
-        chip[h] = (part + sib_recv[h].astype(F32)).astype(BF)
+        for first in range(0, Z * T, step):
+            part = dot(dense[core_rows(c, first), :], feats[h])
+            if first == 0:
+                sib_copy(h).wait_recv()
+            part = part + sib_recv[h, first : first + step].astype(F32)
+            chip[h, first : first + step] = part.astype(BF)
 
     above = jnp.minimum(z + 1, Z - 1)
     below = jnp.maximum(z - 1, 0)
@@ -249,21 +258,21 @@
     def gsib_copy(h, owner):
         r = c * Z + owner
         return remote(
-            grads.at[h, :, tile_at(r)], grads.at[h, :, tile_at(r)], gsib_s.at[h, owner], gsib_r.at[h, owner],
+            grads.at[h, r], grads.at[h, r], gsib_s.at[h, owner], gsib_r.at[h, owner],
             i, sibling,
         )
 
     def gup_copy(h, s):
         r = c * Z + jnp.maximum(z - s, 0)
         return remote(
-            grads.at[h, :, tile_at(r)], grads.at[h, :, tile_at(r)], gup_s.at[h, s], gup_r.at[h, s],
+            grads.at[h, r], grads.at[h, r], gup_s.at[h, s], gup_r.at[h, s],
             i, 2 * above + c,
         )
 
     def gdn_copy(h, s):
         r = c * Z + jnp.minimum(z + s, Z - 1)
         return remote(
-            grads.at[h, :, tile_at(r)], grads.at[h, :, tile_at(r)], gdn_s.at[h, s], gdn_r.at[h, s],
+            grads.at[h, r], grads.at[h, r], gdn_s.at[h, s], gdn_r.at[h, s],
             i, 2 * below + c,
         )
 
@@ -271,7 +280,7 @@
         weight[...], dpre_v[...], (((1,), (1,)), ((), ())), preferred_element_type=F32
     ).astype(BF)
     for h in range(H):
-        grads[h, :, tile_at(c * Z + z)] = turned[h * W : (h + 1) * W, :]
+        grads[h, c * Z + z] = turned[h * W : (h + 1) * W, :]
 
     def give(h):
         send(gup_copy(h, 0), z < Z - 1)
@@ -406,18 +415,21 @@
             lax.rem(i + q, R), j,
         )
 
-    def cell_cols(h, k):
-        return dot(grads[h], dense[:, tile_at(k)])
+    def cell_cols(k):
+        return dot(wide[...], dense[:, tile_at(k)])
 
     def backward(h):
         for d in range(Z):
             gsib_copy(h, d).wait_recv()
-        for q in range(1, R):
-            b_send[h, q - 1] = cell_cols(h, lax.rem(i + q, R)).astype(BF)
+        for r in range(C):
+            wide[:, r * T : (r + 1) * T] = grads[h, r]
+        for q in range(1, R):
+            b_send[h, q - 1] = cell_cols(lax.rem(i + q, R)).astype(BF)
             send(b_copy(h, q))
+        b_own[h] = cell_cols(i)
 
     def total(h):
-        acc = cell_cols(h, i)
+        acc = b_own[h]
         for q in range(1, R):
             b_copy(h, q).wait_recv()
             acc = acc + b_recv[h, q - 1].astype(F32)
@@ -434,16 +446,15 @@
         if wave == 1:
             sum_row()
         h = wave - (Z - 2)
+        if h == H - 1:
+            share_row()
         if h >= 0:
             backward(h)
-            if h == 0:
-                sum_chain()
-            if h == 1:
-                share_row()
-            if h == 2:
-                share_pair()
-            if h >= 1:
-                total(h - 1)
+        if h == 0:
+            sum_chain()
+    for h in range(H - 1):
+        total(h)
+    share_pair()
     total(H - 1)
     w5_copy(1 - c).wait_recv()
 
@@ -484,7 +495,9 @@
         vmem((H, Z - 1, T, W), BF),
         vmem((T, F), BF),
         vmem((T, F), BF),
-        vmem((H, W, C * T), BF),
+        vmem((H, C, W, T), BF),
+        vmem((W, C * T), BF),
+        vmem((H, W, T), F32),
         vmem((H, R - 1, W, T), BF),
         vmem((H, R - 1, W, T), BF),
         vmem((F, F), F32),
@@ -529,7 +542,7 @@
         out_specs=(whole, whole, whole),
         scratch_shapes=scratch,
         compiler_params=pltpu.CompilerParams(
-            collective_id=0, has_side_effects=True, vmem_limit_bytes=60 * 1024 * 1024
+            collective_id=0, has_side_effects=True, vmem_limit_bytes=62 * 1024 * 1024
         ),
         name="layer",
     )(tile_rows, tile_cols, tile_counts, adj_tiles, features, weight, node_grad)

time: 101 us -> 88.4 us (0.88)
  Pallas kernels: 99.6 us -> 87 us
    pallas_call x1, Pallas kernels: 97.2 us -> 84.6 us  [local(): pl.pallas_call(functools.partial(kernel, R, C, scale), out_shape=(jax.Sha...]
where the time goes in v4:
time: 88.4 us; the launch traced here: 88.2 us
  Pallas kernels  87 us (98%)
  between operations  1.29 us (1%)
    pallas_call x1, Pallas kernels, local(): pl.pallas_call(functools.partial(kernel, R, C, scale), out_shape=(jax.Sha...  84.6 us
    pallas_call x1, Pallas kernels, local(): pl.pallas_call(hand_over, out_shape=(jax.ShapeDtypeStruct((T, F), BF), ja...  2.41 us

profile of v4, /device:TPU:0, one launch (start us, length us, event | category | flops | bytes accessed | tf_op | source)
XLA Modules:
  0.0 88.2 jit_solution(14234853990192636481)
XLA Ops:
  1.3 84.6 %layer.1 = (bf16[256,512]{1,0:T(8,128)(2,1)}, bf16[512,512]{1,0:T(8,128)(2,1)}, bf16[256,512]{1,0:T(8,128)(2,1)}) custom-call(s32[1,1,20]{2,1,0:T(1,128)} %rows_s.1, s32[1,1,20]{2,1,0:T(1,128)} %cols_s.1, s32[1,1]{1,0:T(1,128)S(6)} %copy.10.count_s, bf16[1,1,20,256,256]{4,3,2,1,0:T(8,128)(2,1)} %adj_hbm.1, bf16[256,512]{1,0:T(8,128)(2,1)} %feat.1, ...), custom_call_target="tpu_custom_call" | custom-call | tf_op jit(solution)/shard_map/layer/pallas_call | solution.py:534
  85.8 2.4 %hand_over.1 = (bf16[256,512]{1,0:T(8,128)(2,1)}, f32[512,512]{1,0:T(8,128)}, bf16[256,512]{1,0:T(8,128)(2,1)}) custom-call(bf16[256,512]{1,0:T(8,128)(2,1)} %get-tuple-element.6.node_in, bf16[512,512]{1,0:T(8,128)(2,1)} %get-tuple-element.7.weight_in, bf16[256,512]{1,0:T(8,128)(2,1)} %get-tuple-element.8.feature_in), custom_call_target="tpu_custom_call" | custom-call | tf_op jit(solution)/shard_map/hand_over/pallas_call | solution.py:549

commit v5 on v4

--- a/solution.py
+++ b/solution.py
@@ -149,9 +149,8 @@
             j,
         )
 
-    for h in range(H):
-        for q in range(1, R):
-            send(feat_copy(h, q))
+    for q in range(1, R):
+        send(feat_copy(0, q))
 
     adj[slots] = jnp.zeros((T, T), BF)
     adj_copy.wait()
@@ -179,6 +178,9 @@
     def forward(h):
         for q in range(1, R):
             feat_copy(h, q).wait_recv()
+        if h + 1 < H:
+            for q in range(1, R):
+                send(feat_copy(h + 1, q))
         for first in range(0, Z * T, step):
             part = dot(dense[core_rows(1 - c, first), :], feats[h])
             sib_send[h, first : first + step] = part.astype(BF)
@@ -288,7 +290,6 @@
         send(gsib_copy(h, z))
 
     give(0)
-    give(1)
     out[...] = (pre * sigma).astype(BF)
 
     half = F // 2
@@ -435,6 +436,7 @@
             acc = acc + b_recv[h, q - 1].astype(F32)
         fgrad[:, h * W : (h + 1) * W] = acc.T.astype(BF)
 
+    give(1)
     for wave in range(H + Z - 2):
         for s in range(Z - 2, -1, -1):
             if 0 <= wave - s < H:

time: 88.4 us -> 88.8 us (level)
  no operation moved by 1% of the time
where the time goes in v5:
time: 88.8 us; the launch traced here: 88.6 us
  Pallas kernels  87.4 us (98%)
  between operations  1.29 us (1%)
    pallas_call x1, Pallas kernels, local(): pl.pallas_call(functools.partial(kernel, R, C, scale), out_shape=(jax.Sha...  84.9 us
    pallas_call x1, Pallas kernels, local(): pl.pallas_call(hand_over, out_shape=(jax.ShapeDtypeStruct((T, F), BF), ja...  2.41 us

profile of v5, /device:TPU:0, one launch (start us, length us, event | category | flops | bytes accessed | tf_op | source)
XLA Modules:
  0.0 88.6 jit_solution(604521430931332138)
XLA Ops:
  1.3 84.9 %layer.1 = (bf16[256,512]{1,0:T(8,128)(2,1)}, bf16[512,512]{1,0:T(8,128)(2,1)}, bf16[256,512]{1,0:T(8,128)(2,1)}) custom-call(s32[1,1,20]{2,1,0:T(1,128)} %rows_s.1, s32[1,1,20]{2,1,0:T(1,128)} %cols_s.1, s32[1,1]{1,0:T(1,128)S(6)} %copy.10.count_s, bf16[1,1,20,256,256]{4,3,2,1,0:T(8,128)(2,1)} %adj_hbm.1, bf16[256,512]{1,0:T(8,128)(2,1)} %feat.1, ...), custom_call_target="tpu_custom_call" | custom-call | tf_op jit(solution)/shard_map/layer/pallas_call | solution.py:536
  86.2 2.4 %hand_over.1 = (bf16[256,512]{1,0:T(8,128)(2,1)}, f32[512,512]{1,0:T(8,128)}, bf16[256,512]{1,0:T(8,128)(2,1)}) custom-call(bf16[256,512]{1,0:T(8,128)(2,1)} %get-tuple-element.6.node_in, bf16[512,512]{1,0:T(8,128)(2,1)} %get-tuple-element.7.weight_in, bf16[256,512]{1,0:T(8,128)(2,1)} %get-tuple-element.8.feature_in), custom_call_target="tpu_custom_call" | custom-call | tf_op jit(solution)/shard_map/hand_over/pallas_call | solution.py:551
